TPU v7x, 32 devices: a whole 2x2x4 slice. The times are simulated.
32 devices in a mesh: dom: 8 (over y, x, core), feat: 4 (over z).
Axes of the slice: x: 2, y: 2, z: 4, core: 2. Of those that a mesh axis runs over, the one named last changes fastest.
Arguments:
- features: bfloat16 [24576, 1024], P('dom', 'feat'), may hold values from -6 to 6
- w_self: bfloat16 [1024, 256], P('feat'), may hold values from -0.1875 to 0.1875
- w_neigh: bfloat16 [1024, 256], P('feat'), may hold values from -0.1875 to 0.1875
- tile_weights: bfloat16 [192, 20, 128, 128], P(('dom', 'feat')), may hold values from 0.004 to 10.5, as said below
- local_refs: int32 [192, 4], P(('dom', 'feat')), may hold values from 0 to 5
- remote_refs: int32 [192, 16], P(('dom', 'feat')), may hold values from 0 to 95, as said below
- send_tiles: int32 [32, 8, 12], P(('dom', 'feat')), may hold values from 0 to 5
- out_grad: bfloat16 [24576, 256], P(('dom', 'feat')), may hold values from -6 to 6
Outputs:
- hidden: bfloat16 [24576, 256], P(('dom', 'feat'))
- grad_features: bfloat16 [24576, 1024], P('dom', 'feat')
- grad_self: float32 [1024, 256], P('feat')
- grad_neigh: float32 [1024, 256], P('feat')
Inputs may be any that keep to these rules, and one draw needn't show every extreme that they name: For each node block, the 96 entries of remote_refs on its tiles name every received slot exactly once. `tile_weights`: positive edge weights.
All inputs are finite; a program needn't handle non-finite values.
Results may differ from a plain program's by a relative error of at most 0.0062.
Values may be sent and summed in bfloat16 or wider, within the bound.
A program may use at most 128 MiB of HBM per device.

v0:
```python
import jax
import jax.numpy as jnp
from jax import lax
from jax.sharding import PartitionSpec as P


def body(features, w_self, w_neigh, tile_weights, local_refs, remote_refs, send_tiles, out_grad):
    tile_count = tile_weights.shape[0]
    tile_size = tile_weights.shape[2]
    local_count = local_refs.shape[1]
    hidden_width = w_self.shape[1]
    own_count = tile_count * tile_size
    dom_count = lax.axis_size("dom")
    slot_count = send_tiles.shape[2]
    highest = lax.Precision.HIGHEST
    w_both = jnp.concatenate([w_self, w_neigh], axis=1)
    w_full = lax.all_gather(w_both, "feat", axis=0, tiled=True)
    own_rows = lax.all_to_all(features, "feat", split_axis=0, concat_axis=1, tiled=True)
    projected = jnp.dot(own_rows, w_full, preferred_element_type=jnp.float32)
    self_part = projected[:, :hidden_width]
    neigh_tiles = (
        projected[:, hidden_width:]
        .astype(jnp.bfloat16)
        .reshape(tile_count, tile_size, hidden_width)
    )
    outgoing = neigh_tiles[send_tiles[0]]
    incoming = lax.all_to_all(outgoing, "dom", split_axis=0, concat_axis=0, tiled=True)
    received = incoming.reshape(dom_count * slot_count, tile_size, hidden_width)
    sources = jnp.concatenate([neigh_tiles[local_refs], received[remote_refs]], axis=1)
    summed = jnp.einsum("tkij,tkjh->tih", tile_weights, sources, preferred_element_type=jnp.float32)
    degree = jnp.sum(tile_weights, axis=(1, 3), dtype=jnp.float32)
    root_degree = jnp.sqrt(degree)[:, :, None]
    aggregated = (summed / root_degree).reshape(own_count, hidden_width)
    preact = self_part + aggregated
    hidden = jax.nn.silu(preact).astype(jnp.bfloat16)
    logistic = jax.nn.sigmoid(preact)
    grad_pre = out_grad.astype(jnp.float32) * (logistic * (1.0 + preact * (1.0 - logistic)))
    grad_self_rows = grad_pre.astype(jnp.bfloat16)
    grad_agg = (grad_pre.reshape(tile_count, tile_size, hidden_width) / root_degree).astype(
        jnp.bfloat16
    )
    contrib = jnp.einsum(
        "tkij,tih->tkjh", tile_weights, grad_agg, preferred_element_type=jnp.float32
    )
    tile_iota = jnp.arange(tile_count, dtype=jnp.int32)
    local_table = (local_refs[:, :, None] == tile_iota[None, None, :]).astype(jnp.float32)
    local_grads = jnp.einsum(
        "tks,tkjh->sjh", local_table, contrib[:, :local_count], precision=highest
    )
    remote_terms = contrib[:, local_count:].astype(jnp.bfloat16)
    slot_grads = jnp.zeros((dom_count * slot_count, tile_size, hidden_width), jnp.bfloat16)
    slot_grads = slot_grads.at[remote_refs.reshape(-1)].set(
        remote_terms.reshape(-1, tile_size, hidden_width)
    )
    returned = lax.all_to_all(
        slot_grads.reshape(dom_count, slot_count, tile_size, hidden_width),
        "dom",
        split_axis=0,
        concat_axis=0,
        tiled=True,
    )
    send_table = (send_tiles[0][:, :, None] == tile_iota[None, None, :]).astype(jnp.bfloat16)
    remote_grads = jnp.einsum(
        "ibs,ibjh->sjh", send_table, returned, preferred_element_type=jnp.float32
    )
    grad_neigh_nodes = (local_grads + remote_grads).reshape(own_count, hidden_width)
    grad_proj = jnp.concatenate([grad_self_rows, grad_neigh_nodes.astype(jnp.bfloat16)], axis=1)
    piece = lax.all_gather(grad_proj, "feat", axis=0, tiled=True)
    feature_rows = lax.dot_general(
        piece, w_both, (((1,), (1,)), ((), ())), preferred_element_type=jnp.float32
    )
    grad_buffer = feature_rows.astype(jnp.bfloat16)
    weight_running = lax.dot_general(
        features, piece, (((0,), (0,)), ((), ())), preferred_element_type=jnp.float32
    )
    node_total = own_count * dom_count * lax.axis_size("feat")
    grad_w = lax.psum(weight_running, "dom") * float(node_total) ** (-0.5)
    return (hidden, grad_buffer, grad_w[:, :hidden_width], grad_w[:, hidden_width:])


def solution(mesh):
    placed = (
        P("dom", "feat"),
        P("feat", None),
        P("feat", None),
        P(("dom", "feat"), None, None, None),
        P(("dom", "feat"), None),
        P(("dom", "feat"), None),
        P(("dom", "feat"), None, None),
        P(("dom", "feat"), None),
    )
    return jax.shard_map(
        body,
        mesh=mesh,
        in_specs=placed,
        out_specs=(P(("dom", "feat"), None), P("dom", "feat"), P("feat", None), P("feat", None)),
        check_vma=False,
    )
```

profile of v0, /device:TPU:0, one launch (start us, length us, event | category | flops | bytes accessed | tf_op | source)
XLA Modules:
  0.0 430.7 jit_solution(11951104276361419112)
XLA Ops:
  7.2 6.3 %all-to-all-start = ((bf16[4,768,256]{2,1,0:T(8,128)(2,1)}), bf16[4,768,256]{2,1,0:T(8,128)(2,1)S(1)}, u32[]{:S(2)}, u32[]{:S(2)}) async-start(bf16[4,768,256]{2,1,0:T(8,128)(2,1)} %bitcast.71), calls=%async_computation | async-start | bytes 3145728 | tf_op jit(solution)/shard_map/all_to_all | solution.py:18
  17.7 49.6 %all-to-all-done = bf16[4,768,256]{2,1,0:T(8,128)(2,1)S(1)} async-done(((bf16[4,768,256]{2,1,0:T(8,128)(2,1)}), bf16[4,768,256]{2,1,0:T(8,128)(2,1)S(1)}, u32[]{:S(2)}, u32[]{:S(2)}) %all-to-all-start) | async-done | bytes 1572896 | tf_op jit(solution)/shard_map/all_to_all | solution.py:18
  68.0 2.2 convolution_bitcast_fusion.1
  71.7 5.9 %gather_fusion.1 = bf16[96,128,256]{2,1,0:T(8,128)(2,1)} fusion(bf16[6,128,256]{2,1,0:T(8,128)(2,1)S(1)} %bitcast.63, s32[1024]{0:T(1024)S(1)} %get-tuple-element.25), kind=kCustom, calls=%fused_computation.1 | custom fusion | bytes 12583296 | tf_op jit(solution)/shard_map/gather | solution.py:26
  77.6 5.1 %all-to-all-start.1 = ((bf16[8,12,128,256]{3,2,1,0:T(8,128)(2,1)}), bf16[8,12,128,256]{3,2,1,0:T(8,128)(2,1)}, u32[]{:S(2)}, u32[]{:S(2)}) async-start(bf16[8,12,128,256]{3,2,1,0:T(8,128)(2,1)} %bitcast.66), calls=%async_computation.1 | async-start | bytes 12582912 | tf_op jit(solution)/shard_map/all_to_all | solution.py:27
  82.8 2.7 convert_reduce_fusion
  86.4 67.6 %all-to-all-done.1 = bf16[8,12,128,256]{3,2,1,0:T(8,128)(2,1)} async-done(((bf16[8,12,128,256]{3,2,1,0:T(8,128)(2,1)}), bf16[8,12,128,256]{3,2,1,0:T(8,128)(2,1)}, u32[]{:S(2)}, u32[]{:S(2)}) %all-to-all-start.1) | async-done | bytes 6291488 | tf_op jit(solution)/shard_map/all_to_all | solution.py:27
  154.0 8.7 %gather_fusion.2 = bf16[96,128,256]{2,1,0:T(8,128)(2,1)} fusion(bf16[96,128,256]{2,1,0:T(8,128)(2,1)} %bitcast.8, s32[1024]{0:T(1024)S(1)} %pad_clamp_fusion), kind=kCustom, calls=%fused_computation.2 | custom fusion | bytes 12583296 | tf_op jit(solution)/shard_map/gather | solution.py:29
  162.8 5.5 %fusion.18 = f32[6,256,128]{1,2,0:T(8,128)S(1)} fusion(bf16[6,20,128,128]{3,2,1,0:T(8,128)(2,1)} %param.11, bf16[6,16,128,256]{3,2,1,0:T(8,128)(2,1)} %bitcast.68, bf16[6,4,128,256]{3,2,1,0:T(8,128)(2,1)S(1)} %bitcast.72, f32[6,128]{1,0:T(8,128)S(1)} %sqrt.7), kind=kOutput, calls=%fused_computation.28 | convolution fusion | flops 1022558208 | bytes 12585984 | tf_op jit(solution)/shard_map/tkij,tkjh->tih/dot_general | solution.py:30
  168.6 2.3 fusion.30
  171.1 9.9 %convolution_bitcast_fusion = f32[6,20,128,256]{2,3,1,0:T(8,128)} fusion(bf16[6,20,128,128]{3,2,1,0:T(8,128)(2,1)} %param.11, f32[6,128,256]{2,1,0:T(8,128)S(1)} %bitcast.70, f32[6,128]{1,0:T(8,128)S(1)} %sqrt.7), kind=kOutput, calls=%fused_computation.12 | convolution fusion | flops 1007026176 | bytes 20450304 | tf_op jit(solution)/shard_map/tkij,tih->tkjh/dot_general | solution.py:42
  181.0 8.6 %slice.45 = bf16[6,16,128,256]{2,3,1,0:T(8,128)(2,1)} slice(f32[6,20,128,256]{2,3,1,0:T(8,128)} %convolution_bitcast_fusion), slice={[0:6], [4:20], [0:128], [0:256]} | slice | bytes 12582912 | tf_op jit(solution)/shard_map/slice | solution.py:50
  189.6 8.6 %copy.59 = bf16[96,128,256]{2,1,0:T(8,128)(2,1)} copy(bf16[96,128,256]{1,2,0:T(8,128)(2,1)} %bitcast.67) | data formatting | bytes 12582912 | tf_op jit(solution)/shard_map/reshape | solution.py:53
  198.2 3.5 broadcast_in_dim.8
  201.7 17.6 %scatter_fusion = bf16[96,128,256]{2,1,0:T(8,128)(2,1)} fusion(bf16[96,128,256]{2,1,0:T(8,128)(2,1)} %broadcast_in_dim.8, s32[96]{0:T(128)S(1)} %fusion.28, bf16[96,128,256]{2,1,0:T(8,128)(2,1)} %copy.59), kind=kCustom, calls=%fused_computation.3 | custom fusion | bytes 18874752 | tf_op jit(solution)/shard_map/scatter | solution.py:52
  219.3 4.7 %all-to-all-start.2 = ((bf16[8,12,128,256]{3,2,1,0:T(8,128)(2,1)}), bf16[8,12,128,256]{3,2,1,0:T(8,128)(2,1)}, u32[]{:S(2)}, u32[]{:S(2)}) async-start(bf16[8,12,128,256]{3,2,1,0:T(8,128)(2,1)} %bitcast.65), calls=%async_computation.2 | async-start | bytes 12582912 | tf_op jit(solution)/shard_map/all_to_all | solution.py:55
  226.0 3.4 copy.58
  229.4 4.1 convolution_bitcast_fusion.2
  233.5 62.2 %all-to-all-done.2 = bf16[8,12,128,256]{3,2,1,0:T(8,128)(2,1)} async-done(((bf16[8,12,128,256]{3,2,1,0:T(8,128)(2,1)}), bf16[8,12,128,256]{3,2,1,0:T(8,128)(2,1)}, u32[]{:S(2)}, u32[]{:S(2)}) %all-to-all-start.2) | async-done | bytes 6291488 | tf_op jit(solution)/shard_map/all_to_all | solution.py:55
  295.7 6.5 %fusion.12 = bf16[6,128,256]{2,0,1:T(8,128)(2,1)S(1)} fusion(f32[6,128,256]{2,0,1:T(8,128)S(1)} %convolution_bitcast_fusion.2, bf16[8,12,128,256]{3,2,1,0:T(8,128)(2,1)} %all-to-all-done.2, s32[8,12]{1,0:T(8,128)S(1)} %bitcast.76), kind=kOutput, calls=%fused_computation.18 | convolution fusion | flops 38142528 | bytes 7471488 | tf_op jit(solution)/shard_map/ibs,ibjh->sjh/dot_general | solution.py:63
  304.3 60.0 %all-gather.5.cloned.1.call-done = bf16[3072,512]{0,1:T(8,128)(2,1)} async-done(((bf16[768,512]{0,1:T(8,128)(2,1)}), bf16[3072,512]{0,1:T(8,128)(2,1)}) %all-gather.5.cloned.1.call-update) | async-done | bytes 3145744 | tf_op jit(solution)/shard_map/all_gather | solution.py:68
  364.3 3.7 convolution_bitcast_fusion.3
  368.0 4.1 convolution_convert_fusion
  372.1 49.3 %all-reduce.2.cloned.1.call-done = f32[256,512]{0,1:T(8,128)} async-done(((f32[256,512]{0,1:T(8,128)}), f32[256,512]{0,1:T(8,128)}) %all-reduce.2.cloned.1.call-update) | async-done | bytes 524304 | tf_op jit(solution)/shard_map/psum | solution.py:77
  (56 shorter events, 14.6 us)
Async XLA Ops:
  7.2 60.1 %all-to-all-start = ((bf16[4,768,256]{2,1,0:T(8,128)(2,1)}), bf16[4,768,256]{2,1,0:T(8,128)(2,1)S(1)}, u32[]{:S(2)}, u32[]{:S(2)}) async-start(bf16[4,768,256]{2,1,0:T(8,128)(2,1)} %bitcast.71), calls=%async_computation | async-start | bytes 3145728 | tf_op jit(solution)/shard_map/all_to_all | solution.py:18
  13.5 54.5 %all-gather.3.cloned.1.call-start = ((), (), s32[]{:S(2)}) async-start(), calls=%async_computation.3 | async-start | bytes 1310720 | tf_op jit(solution)/shard_map/all_gather | solution.py:17
  15.3 0.7 copy-start.3
  70.3 1.1 copy-start.2
  77.6 5.1 %copy-start.6 = (s32[6,16]{1,0:T(8,128)S(1)}, s32[6,16]{1,0:T(8,128)}, u32[]{:S(2)}) copy-start(s32[6,16]{1,0:T(8,128)} %param.13) | copy-start | bytes 1156
  77.6 76.5 %all-to-all-start.1 = ((bf16[8,12,128,256]{3,2,1,0:T(8,128)(2,1)}), bf16[8,12,128,256]{3,2,1,0:T(8,128)(2,1)}, u32[]{:S(2)}, u32[]{:S(2)}) async-start(bf16[8,12,128,256]{3,2,1,0:T(8,128)(2,1)} %bitcast.66), calls=%async_computation.1 | async-start | bytes 12582912 | tf_op jit(solution)/shard_map/all_to_all | solution.py:27
  82.6 2.9 copy-start.5
  219.3 76.3 %all-to-all-start.2 = ((bf16[8,12,128,256]{3,2,1,0:T(8,128)(2,1)}), bf16[8,12,128,256]{3,2,1,0:T(8,128)(2,1)}, u32[]{:S(2)}, u32[]{:S(2)}) async-start(bf16[8,12,128,256]{3,2,1,0:T(8,128)(2,1)} %bitcast.65), calls=%async_computation.2 | async-start | bytes 12582912 | tf_op jit(solution)/shard_map/all_to_all | solution.py:55
  224.1 1.9 slice-start
  224.1 140.2 %all-gather.5.cloned.1.call-start = ((), (), s32[]{:S(2)}) async-start(), calls=%async_computation.4 | async-start | bytes 3932160 | tf_op jit(solution)/shard_map/all_gather | solution.py:68
  226.0 3.4 copy-start.7
  229.4 66.3 %copy-start.8 = (s32[1,8,12]{2,1,0:T(8,128)S(1)}, s32[1,8,12]{2,1,0:T(8,128)}, u32[]{:S(2)}) copy-start(s32[1,8,12]{2,1,0:T(8,128)} %param.14) | copy-start | bytes 1156
  295.7 6.7 %copy-start.1 = (bf16[768,256]{0,1:T(8,128)(2,1)S(1)}, bf16[768,256]{0,1:T(8,128)(2,1)}, u32[]{:S(2)}) copy-start(bf16[768,256]{0,1:T(8,128)(2,1)} %get-tuple-element.20) | copy-start | bytes 1179652
  302.1 62.2 %copy-start = (bf16[3072,256]{1,0:T(8,128)(2,1)S(1)}, bf16[3072,256]{1,0:T(8,128)(2,1)}, u32[]{:S(2)}) copy-start(bf16[3072,256]{1,0:T(8,128)(2,1)} %param.8) | copy-start | bytes 4718596
  303.3 64.6 %copy-start.4 = (bf16[256,512]{1,0:T(8,128)(2,1)S(1)}, bf16[256,512]{1,0:T(8,128)(2,1)}, u32[]{:S(2)}) copy-start(bf16[256,512]{1,0:T(8,128)(2,1)} %copy-done.3) | copy-start | bytes 786436
  303.4 118.0 %all-reduce.2.cloned.1.call-start = ((), (), s32[]{:S(2)}) async-start(), calls=%async_computation.5 | async-start | bytes 1048576 | tf_op jit(solution)/shard_map/psum | solution.py:77
Sparse Core Ops, SparseCore 0:
  16.5 45.4 all-gather.2
  303.5 60.7 all-gather.4
  368.1 53.2 all-reduce.1
where the time goes:
time: 432 us; the launch traced here: 431 us
  waiting for transfers between devices  289 us (67%)
  local copies, waits for them, and re-layouts  67.2 us (16%)
  matrix products  35.9 us (8%)
  starting transfers between devices  16.4 us (4%)
  between operations  14 us (3%)
  other arithmetic  8.38 us (2%)
    all_to_all x1, waiting for transfers between devices, body(): lax.all_to_all(outgoing, 'dom', split_axis=0, concat_axis=0, tiled=True)  67.6 us
    all_to_all x1, waiting for transfers between devices, body(): lax.all_to_all(slot_grads.reshape(dom_count, slot_count, tile_size, hidde...  62.2 us
    all_gather x1, waiting for transfers between devices, body(): piece = lax.all_gather(grad_proj, 'feat', axis=0, tiled=True)  60 us
    all_to_all x1, waiting for transfers between devices, body(): lax.all_to_all(features, 'feat', split_axis=0, concat_axis=1, tiled=True)  49.6 us
    psum x1, waiting for transfers between devices, body(): grad_w = lax.psum(weight_running, 'dom') * float(node_total) ** (-0.5)  49.3 us
    scatter x1, local copies, waits for them, and re-layouts, body(): slot_grads.at[remote_refs.reshape(-1)]  17.6 us
    dot_general x1, matrix products, body(): jnp.einsum('tkij,tih->tkjh', tile_weights, grad_agg, preferred_element_ty...  9.91 us
    gather x1, local copies, waits for them, and re-layouts, body(): received[remote_refs]  8.74 us
  transfers between devices with their start and end apart: 6, of which 5 were waited for; matrix products, arithmetic and copies ran while one was open for 5% of the time, Pallas kernels for 0%

commit v1 on v0

v1 whole, which is shorter than its diff:
```python
import functools
import math

import jax
import jax.numpy as jnp
from jax import lax
from jax.experimental import pallas as pl
from jax.experimental.pallas import tpu as pltpu
from jax.sharding import PartitionSpec as P

MESH = pl.DeviceIdType.MESH
F32 = jnp.float32
BF16 = jnp.bfloat16
LANES = 8
HALVES = 2
ORDERS = 2
VMEM_LIMIT = 60 * 1024 * 1024


def send(src, dst, send_sem, recv_sem, where):
    copy = pltpu.make_async_remote_copy(
        src_ref=src, dst_ref=dst, send_sem=send_sem, recv_sem=recv_sem,
        device_id=where, device_id_type=MESH,
    )
    copy.start()
    return copy


def arrived(ref, sem):
    pltpu.make_async_remote_copy(
        src_ref=ref, dst_ref=ref, send_sem=sem, recv_sem=sem,
        device_id={"feat": lax.axis_index("feat")}, device_id_type=MESH,
    ).wait_recv()


def greet(dom_count, feat_count):
    d, z = lax.axis_index("dom"), lax.axis_index("feat")
    barrier = pltpu.get_barrier_semaphore()
    for i in range(1, dom_count):
        pl.semaphore_signal(
            barrier, inc=1, device_id={"dom": lax.rem(d + i, dom_count)}, device_id_type=MESH
        )
    for i in range(1, feat_count):
        pl.semaphore_signal(
            barrier, inc=1, device_id={"feat": lax.rem(z + i, feat_count)}, device_id_type=MESH
        )
    pl.semaphore_wait(barrier, dom_count + feat_count - 2)


def rows_at(start, size, unit):
    return pl.ds(pl.multiple_of(start, unit), size)


def project_kernel(
    sizes, features, w_self, w_neigh, slots, own, w_full, self_part, gathered, table,
    local_sem, w1s, w1r, w2s, w2r, fs, fr, ts, tr, s1, s2, s3, agr,
):
    dom_count, nf, rows, fl, hidden, n = sizes
    d, z = lax.axis_index("dom"), lax.axis_index("feat")
    core = lax.rem(d, 2)
    chip = d // 2
    x, y = lax.rem(chip, n), chip // n
    lane = lax.rem(d, LANES)
    base = d - lane
    wr = fl // LANES
    half = rows // HALVES
    piece = half // ORDERS
    greet(dom_count, nf)
    sends = []
    w_full[z, :, :hidden] = w_self[...]
    w_full[z, :, hidden:] = w_neigh[...]
    mine = rows_at(lane * wr, wr, wr)
    for i in range(1, nf):
        zt = lax.rem(z + i, nf)
        ref = w_full.at[z, mine, :]
        sends.append(send(ref, ref, w1s.at[i], w1r.at[z], {"feat": zt}))
    local = pltpu.make_async_copy(features.at[rows_at(z * rows, rows, rows), :], own.at[z], local_sem)
    local.start()
    for h in range(HALVES):
        for i in range(nf - 1, 0, -1):
            zt = lax.rem(z + i, nf)
            sends.append(send(
                features.at[rows_at(zt * rows + h * half, half, half), :],
                own.at[z, pl.ds(h * half, half), :],
                fs.at[h, i], fr.at[h, z], {"feat": zt},
            ))
    for i in range(1, dom_count):
        to = lax.rem(d + i, dom_count)
        sends.append(send(slots.at[to], table.at[d], ts.at[i], tr.at[d], {"dom": to}))
    table[d] = slots[d]
    for i in range(1, nf):
        zs = lax.rem(z + i, nf)
        ref = w_full.at[zs, mine, :]
        arrived(ref, w1r.at[zs])
        for j in range(1, LANES):
            to = base + lax.rem(lane + j, LANES)
            sends.append(send(ref, ref, w2s.at[i, j], w2r.at[zs, lane], {"dom": to}))
    for i in range(1, nf):
        zs = lax.rem(z + i, nf)
        for j in range(1, LANES):
            other = lax.rem(lane + j, LANES)
            arrived(w_full.at[zs, rows_at(other * wr, wr, wr), :], w2r.at[zs, other])
    local.wait()

    def place(order, first, second, which):
        if order == 0:
            return (second * n + first) * 2 + which
        return (first * n + second) * 2 + which

    for h in range(HALVES):
        span = pl.ds(h * half, half)
        for i in range(1, nf):
            zs = lax.rem(z + i, nf)
            arrived(own.at[zs, span, :], fr.at[h, zs])

        total = jnp.dot(own[0, span, :], w_full[0], preferred_element_type=F32)
        for k in range(1, nf):
            total += jnp.dot(own[k, span, :], w_full[k], preferred_element_type=F32)
        self_part[span, :] = total[:, :hidden]
        gathered[d, span, :] = total[:, hidden:].astype(BF16)

        def spread(block, c, sems, to):
            ref = gathered.at[block, pl.ds(c * piece, piece), :]
            sends.append(send(ref, ref, sems, agr.at[block, c], {"dom": to}))

        def came(block, c):
            arrived(gathered.at[block, pl.ds(c * piece, piece), :], agr.at[block, c])

        steps = []
        for o in range(ORDERS):
            c = h * ORDERS + o
            p1, p2 = (x, y) if o == 0 else (y, x)
            at = lambda i1, i2, which, o=o, p1=p1, p2=p2: place(
                o, lax.rem(p1 + i1, n), lax.rem(p2 + i2, n), which
            )
            steps.append((c, at))
        for c, at in steps:
            for i in range(1, n):
                spread(d, c, s1.at[c, i], at(i, 0, core))
            for i in range(1, n):
                spread(d, c, s2.at[c, 0, i], at(0, i, core))
            spread(d, c, s3.at[c, 0, 0], at(0, 0, 1 - core))
        for c, at in steps:
            for i1 in range(1, n):
                block = at(i1, 0, core)
                came(block, c)
                for i2 in range(1, n):
                    spread(block, c, s2.at[c, i1, i2], at(0, i2, core))
                spread(block, c, s3.at[c, i1, 0], at(0, 0, 1 - core))
        for c, at in steps:
            for i2 in range(1, n):
                for i1 in range(n):
                    block = at(i1, i2, core)
                    came(block, c)
                    spread(block, c, s3.at[c, i1, i2], at(0, 0, 1 - core))
    for c in range(HALVES * ORDERS):
        for b in range(dom_count // 2):
            block = b * 2 + 1 - core
            arrived(gathered.at[block, pl.ds(c * piece, piece), :], agr.at[block, c])
    for i in range(1, dom_count):
        other = lax.rem(d + i, dom_count)
        arrived(table.at[other], tr.at[other])
    for copy in sends:
        copy.wait_send()


def aggregate_kernel(
    sizes, local_refs, remote_refs, table, weights, self_part, out_grad, gathered,
    hidden_out, grad_self, partial, acc,
):
    dom_count, local_count, count, slot_count, tile, chips = sizes
    t = pl.program_id(0)
    d = lax.axis_index("dom")

    @pl.when(t == 0)
    def _():
        def clear(b, carry):
            acc[b] = jnp.zeros(acc.shape[1:], F32)
            return carry
        lax.fori_loop(0, dom_count, clear, 0)

    blocks, spans = [], []
    for k in range(count):
        if k < local_count:
            r, u = d, local_refs[t, k]
        else:
            q = remote_refs[t, k - local_count]
            r = q // slot_count
            u = table[r, q - r * slot_count]
        blocks.append(r)
        spans.append(rows_at(u * tile, tile, tile))
    degree = jnp.zeros((tile, tile), F32)
    summed = jnp.zeros((tile, gathered.shape[2]), F32)
    for k in range(0, count, 2):
        pair = range(k, min(k + 2, count))
        left = [weights[0, j] for j in pair]
        for w in left:
            degree += w.astype(F32)
        right = [gathered[blocks[j], spans[j], :] for j in pair]
        summed += jnp.dot(
            jnp.concatenate(left, axis=1), jnp.concatenate(right, axis=0),
            preferred_element_type=F32,
        )
    root = jnp.sqrt(jnp.sum(degree, axis=1, keepdims=True))
    preact = self_part[...] + summed / root
    logistic = jax.nn.sigmoid(preact)
    hidden_out[...] = (preact * logistic).astype(BF16)
    grad_pre = out_grad[...].astype(F32) * (logistic * (1.0 + preact * (1.0 - logistic)))
    grad_self[...] = grad_pre.astype(BF16)
    grad_agg = (grad_pre / root).astype(BF16)
    for k in range(count):
        contrib = lax.dot_general(
            weights[0, k], grad_agg, (((0,), (0,)), ((), ())), preferred_element_type=F32
        )
        at = lax.rem(blocks[k], 2) * chips + blocks[k] // 2
        acc[at, spans[k], :] += contrib

    @pl.when(t == pl.num_programs(0) - 1)
    def _():
        def finish(b, carry):
            partial[b] = acc[b].astype(BF16)
            return carry
        lax.fori_loop(0, dom_count, finish, 0)


def reduce_kernel(
    sizes, scale, partial, grad_self, own, w_full, grad_out, gw_self, gw_neigh,
    from_sib, sums, b1, b2, grad_proj, stage, gw, gw_recv, gw_sum, gw_cross, gw_z,
    local_sem, ss, sr, as1, ar1, as2, ar2, zs_, zr, g1s, g1r, gcs, gcr, g2s, g2r, g3s, g3r,
):
    dom_count, nf, rows, fl, hidden, n = sizes
    d, z = lax.axis_index("dom"), lax.axis_index("feat")
    core = lax.rem(d, 2)
    chip = d // 2
    x, y = lax.rem(chip, n), chip // n
    lane = lax.rem(d, LANES)
    base = d - lane
    wr = fl // LANES
    chunks = HALVES * ORDERS
    piece = rows // chunks
    groups = dom_count // LANES
    greet(dom_count, nf)
    sends, locals_ = [], []
    for c in range(chunks):
        span = pl.ds(c * piece, piece)
        sends.append(send(
            partial.at[1 - core, :, :, span, :], from_sib.at[:, :, span, :],
            ss.at[c], sr.at[c], {"dom": chip * 2 + 1 - core},
        ))
    grad_proj[:, :hidden] = grad_self[...]
    for c in range(chunks):
        span = pl.ds(c * piece, piece)
        arrived(from_sib.at[:, :, span, :], sr.at[c])
        for yy in range(n):
            for xx in range(n):
                sums[yy, xx, span, :] = (
                    partial[core, yy, xx, span, :].astype(F32)
                    + from_sib[yy, xx, span, :].astype(F32)
                ).astype(BF16)
        for i in range(1, n):
            if c % ORDERS == 0:
                xt = lax.rem(x + i, n)
                src, me, to = sums.at[:, xt, span, :], x, (y * n + xt) * 2 + core
            else:
                yt = lax.rem(y + i, n)
                src, me, to = sums.at[yt, :, span, :], y, (yt * n + x) * 2 + core
            sends.append(send(src, b1.at[me, :, span, :], as1.at[c, i], ar1.at[c, me], {"dom": to}))
    for c in range(chunks):
        span = pl.ds(c * piece, piece)
        me1, me2 = (x, y) if c % ORDERS == 0 else (y, x)
        for i in range(1, n):
            other = lax.rem(me1 + i, n)
            arrived(b1.at[other, :, span, :], ar1.at[c, other])
        for j in range(n):
            to2 = lax.rem(me2 + j, n)
            if c % ORDERS == 0:
                total = sums[to2, x, span, :].astype(F32)
            else:
                total = sums[y, to2, span, :].astype(F32)
            for i in range(1, n):
                total += b1[lax.rem(me1 + i, n), to2, span, :].astype(F32)
            b1[me1, to2, span, :] = total.astype(BF16)
            if j:
                to = ((to2 * n + x) if c % ORDERS == 0 else (y * n + to2)) * 2 + core
                sends.append(send(
                    b1.at[me1, to2, span, :], b2.at[me2, span, :], as2.at[c, j], ar2.at[c, me2],
                    {"dom": to},
                ))
    for c in range(chunks):
        span = pl.ds(c * piece, piece)
        me1, me2 = (x, y) if c % ORDERS == 0 else (y, x)
        total = b1[me1, me2, span, :].astype(F32)
        for i in range(1, n):
            other = lax.rem(me2 + i, n)
            arrived(b2.at[other, span, :], ar2.at[c, other])
            total += b2[other, span, :].astype(F32)
        grad_proj[span, hidden:] = total.astype(BF16)
        for i in range(nf - 1, -1, -1):
            zt = lax.rem(z + i, nf)
            stage[zt, span, :] = lax.dot_general(
                grad_proj[span, :], w_full[zt], (((1,), (1,)), ((), ())),
                preferred_element_type=F32,
            ).astype(BF16)
            target = grad_out.at[rows_at(z * rows + c * piece, piece, piece), :]
            if i:
                sends.append(send(
                    stage.at[zt, span, :], target, zs_.at[c, i], zr.at[c, z], {"feat": zt}
                ))
            else:
                copy = pltpu.make_async_copy(stage.at[zt, span, :], target, local_sem.at[c])
                copy.start()
                locals_.append(copy)
    for k in range(nf):
        gw[k] = lax.dot_general(
            own[k], grad_proj[...], (((0,), (0,)), ((), ())), preferred_element_type=F32
        ).astype(BF16)
    mine = rows_at(lane * wr, wr, wr)
    for j in range(1, LANES):
        other = lax.rem(lane + j, LANES)
        sends.append(send(
            gw.at[:, rows_at(other * wr, wr, wr), :], gw_recv.at[lane], g1s.at[j], g1r.at[lane],
            {"dom": base + other},
        ))
    total = gw[:, mine, :].astype(F32)
    for j in range(1, LANES):
        other = lax.rem(lane + j, LANES)
        arrived(gw_recv.at[other], g1r.at[other])
        total += gw_recv[other].astype(F32)
    gw_sum[...] = total
    if groups > 1:
        group = d // LANES
        gw_cross[group] = gw_sum[...]
        for j in range(1, groups):
            sends.append(send(
                gw_cross.at[group], gw_cross.at[group], gcs.at[j], gcr.at[group],
                {"dom": lax.rem(d + j * LANES, dom_count)},
            ))
        for j in range(1, groups):
            other = lax.rem(group + j, groups)
            arrived(gw_cross.at[other], gcr.at[other])
            total += gw_cross[other]
        gw_sum[...] = total
    for i in range(1, nf):
        zt = lax.rem(z + i, nf)
        sends.append(send(gw_sum.at[zt], gw_z.at[z], g2s.at[i], g2r.at[z], {"feat": zt}))
    final = gw_sum[z]
    for i in range(1, nf):
        zt = lax.rem(z + i, nf)
        arrived(gw_z.at[zt], g2r.at[zt])
        final += gw_z[zt]
    final = final * scale
    gw_self[mine, :] = final[:, :hidden]
    gw_neigh[mine, :] = final[:, hidden:]
    for j in range(1, LANES):
        to = {"dom": base + lax.rem(lane + j, LANES)}
        for which, ref in enumerate((gw_self, gw_neigh)):
            at = ref.at[mine, :]
            sends.append(send(at, at, g3s.at[which, j], g3r.at[which, lane], to))
    for j in range(1, LANES):
        other = lax.rem(lane + j, LANES)
        for which, ref in enumerate((gw_self, gw_neigh)):
            arrived(ref.at[rows_at(other * wr, wr, wr), :], g3r.at[which, other])
    for c in range(chunks):
        for i in range(1, nf):
            zt = lax.rem(z + i, nf)
            arrived(grad_out.at[rows_at(zt * rows + c * piece, piece, piece), :], zr.at[c, zt])
    for copy in locals_:
        copy.wait()
    for copy in sends:
        copy.wait_send()


def body(features, w_self, w_neigh, tile_weights, local_refs, remote_refs, send_tiles, out_grad):
    tile_count, count, tile = tile_weights.shape[:3]
    local_count = local_refs.shape[1]
    fl, hidden = w_self.shape
    rows = tile_count * tile
    dom_count, nf = lax.axis_size("dom"), lax.axis_size("feat")
    slot_count = send_tiles.shape[2]
    n = math.isqrt(dom_count // 2)
    chips = n * n
    chunks = HALVES * ORDERS
    node_total = rows * dom_count * nf
    vmem = pl.BlockSpec(memory_space=pltpu.VMEM)
    smem = pl.BlockSpec(memory_space=pltpu.SMEM)
    hbm = pl.BlockSpec(memory_space=pl.ANY)
    dma = pltpu.SemaphoreType.DMA
    sizes = (dom_count, nf, rows, fl, hidden, n)
    slots = jnp.zeros((dom_count, 8, 128), jnp.int32).at[:, 0, :slot_count].set(send_tiles[0])
    own, w_full, self_part, gathered, table = pl.pallas_call(
        functools.partial(project_kernel, sizes),
        out_shape=(
            jax.ShapeDtypeStruct((nf, rows, fl), BF16),
            jax.ShapeDtypeStruct((nf, fl, 2 * hidden), BF16),
            jax.ShapeDtypeStruct((rows, hidden), F32),
            jax.ShapeDtypeStruct((dom_count, rows, hidden), BF16),
            jax.ShapeDtypeStruct((dom_count, 8, 128), jnp.int32),
        ),
        in_specs=[hbm, vmem, vmem, vmem],
        out_specs=(vmem,) * 5,
        scratch_shapes=[
            dma, dma((nf,)), dma((nf,)), dma((nf, LANES)), dma((nf, LANES)),
            dma((HALVES, nf)), dma((HALVES, nf)), dma((dom_count,)), dma((dom_count,)),
            dma((chunks, n)), dma((chunks, n, n)), dma((chunks, n, n)), dma((dom_count, chunks)),
        ],
        compiler_params=pltpu.CompilerParams(
            collective_id=0, has_side_effects=True, vmem_limit_bytes=VMEM_LIMIT
        ),
    )(features, w_self, w_neigh, slots)

    hidden_out, grad_self, partial = pl.pallas_call(
        functools.partial(
            aggregate_kernel, (dom_count, local_count, count, slot_count, tile, chips)
        ),
        grid=(tile_count,),
        out_shape=(
            jax.ShapeDtypeStruct((rows, hidden), BF16),
            jax.ShapeDtypeStruct((rows, hidden), BF16),
            jax.ShapeDtypeStruct((dom_count, rows, hidden), BF16),
        ),
        in_specs=[
            smem, smem, smem,
            pl.BlockSpec((1, count, tile, tile), lambda t: (t, 0, 0, 0)),
            pl.BlockSpec((tile, hidden), lambda t: (t, 0)),
            pl.BlockSpec((tile, hidden), lambda t: (t, 0)),
            vmem,
        ],
        out_specs=(
            pl.BlockSpec((tile, hidden), lambda t: (t, 0)),
            pl.BlockSpec((tile, hidden), lambda t: (t, 0)),
            vmem,
        ),
        scratch_shapes=[pltpu.VMEM((dom_count, rows, hidden), F32)],
        compiler_params=pltpu.CompilerParams(vmem_limit_bytes=VMEM_LIMIT),
    )(local_refs, remote_refs, table[:, 0, :slot_count], tile_weights, self_part, out_grad, gathered)

    wr = fl // LANES
    groups = dom_count // LANES
    grad_out, gw_self, gw_neigh = pl.pallas_call(
        functools.partial(reduce_kernel, sizes, float(node_total) ** (-0.5)),
        out_shape=(
            jax.ShapeDtypeStruct((nf * rows, fl), BF16),
            jax.ShapeDtypeStruct((fl, hidden), F32),
            jax.ShapeDtypeStruct((fl, hidden), F32),
        ),
        in_specs=[vmem] * 4,
        out_specs=(hbm, vmem, vmem),
        scratch_shapes=[
            pltpu.VMEM((n, n, rows, hidden), BF16),
            pltpu.VMEM((n, n, rows, hidden), BF16),
            pltpu.VMEM((n, n, rows, hidden), BF16),
            pltpu.VMEM((n, rows, hidden), BF16),
            pltpu.VMEM((rows, 2 * hidden), BF16),
            pltpu.VMEM((nf, rows, fl), BF16),
            pltpu.VMEM((nf, fl, 2 * hidden), BF16),
            pltpu.VMEM((LANES, nf, wr, 2 * hidden), BF16),
            pltpu.VMEM((nf, wr, 2 * hidden), F32),
            pltpu.VMEM((groups, nf, wr, 2 * hidden), F32),
            pltpu.VMEM((nf, wr, 2 * hidden), F32),
            dma((chunks,)), dma((chunks,)), dma((chunks,)),
            dma((chunks, n)), dma((chunks, n)), dma((chunks, n)), dma((chunks, n)),
            dma((chunks, nf)), dma((chunks, nf)),
            dma((LANES,)), dma((LANES,)), dma((groups,)), dma((groups,)),
            dma((nf,)), dma((nf,)), dma((2, LANES)), dma((2, LANES)),
        ],
        compiler_params=pltpu.CompilerParams(
            collective_id=1, has_side_effects=True, vmem_limit_bytes=VMEM_LIMIT
        ),
    )(partial.reshape(2, n, n, rows, hidden), grad_self, own, w_full)
    return (hidden_out, grad_out, gw_self, gw_neigh)


def solution(mesh):
    placed = (
        P("dom", "feat"),
        P("feat", None),
        P("feat", None),
        P(("dom", "feat"), None, None, None),
        P(("dom", "feat"), None),
        P(("dom", "feat"), None),
        P(("dom", "feat"), None, None),
        P(("dom", "feat"), None),
    )
    return jax.shard_map(
        body,
        mesh=mesh,
        in_specs=placed,
        out_specs=(P(("dom", "feat"), None), P("dom", "feat"), P("feat", None), P("feat", None)),
        check_vma=False,
    )
```

time: 432 us -> 150 us (0.35)
  waiting for transfers between devices: 289 us -> 0 us
  Pallas kernels: 0 us -> 141 us
  local copies, waits for them, and re-layouts: 67.2 us -> 8.13 us
  matrix products: 35.9 us -> 0 us
  starting transfers between devices: 16.4 us -> 0 us
  between operations: 14 us -> 0.67 us
  other arithmetic: 8.38 us -> 0 us
    all_to_all x3 -> x0, waiting for transfers between devices: 179 us -> none  [the longest x1 67.6 us: body(): lax.all_to_all(outgoing, 'dom', split_axis=0, concat_axis=0, tiled=True)]
    pallas_call x0 -> x3, Pallas kernels: none -> 141 us  [the longest x1 68 us: body(): pl.pallas_call(functools.partial(reduce_kernel, sizes, float(node_total)...]
    all_gather x2 -> x0, waiting for transfers between devices: 60 us -> none  [the longest x1 60 us: body(): piece = lax.all_gather(grad_proj, 'feat', axis=0, tiled=True)]
    psum x1 -> x0, waiting for transfers between devices: 49.3 us -> none  [body(): grad_w = lax.psum(weight_running, 'dom') * float(node_total) ** (-0.5)]
    dot_general x7 -> x0, matrix products: 35.9 us -> none  [the longest x1 9.91 us: body(): jnp.einsum('tkij,tih->tkjh', tile_weights, grad_agg, preferred_element_ty...]
    scatter x1, local copies, waits for them, and re-layouts: 17.6 us -> 1.31 us  [body(): jnp.zeros((dom_count, 8, 128), jnp.int32).at[:, 0, :slot_count]]
    all_to_all x3 -> x0, starting transfers between devices: 16.1 us -> none  [the longest x1 6.33 us: body(): lax.all_to_all(features, 'feat', split_axis=0, concat_axis=1, tiled=True)]
    gather x3 -> x0, local copies, waits for them, and re-layouts: 15.3 us -> none  [the longest x1 8.74 us: body(): received[remote_refs]]
  transfers between devices with their start and end apart: 6 -> 0, of which waited for: 5 -> 0; matrix products, arithmetic and copies ran while one was open for 5% -> 0% of each run, Pallas kernels for 0% -> 0%
where the time goes in v1:
time: 150 us
  Pallas kernels  141 us (94%)
  local copies, waits for them, and re-layouts  8.13 us (5%)
    pallas_call x1, Pallas kernels, body(): pl.pallas_call(functools.partial(reduce_kernel, sizes, float(node_total)...  68 us
    pallas_call x1, Pallas kernels, body(): pl.pallas_call(functools.partial(project_kernel, sizes), out_shape=(jax.S...  61.1 us
    pallas_call x1, Pallas kernels, body(): pl.pallas_call(functools.partial(aggregate_kernel, (dom_count, local_coun...  12.1 us
    unnamed x8, local copies, waits for them, and re-layouts  5.47 us

profile of v1, /device:TPU:0, one launch (start us, length us, event | category | flops | bytes accessed | tf_op | source)
XLA Modules:
  0.0 150.0 jit_solution(3560567151305911517)
XLA Ops:
  0.6 1.4 copy.13.local_refs
  2.0 1.3 scatter.4.slots
  3.3 61.1 %shard_map.111 = (bf16[4,768,256]{2,1,0:T(8,128)(2,1)}, bf16[4,256,512]{2,1,0:T(8,128)(2,1)}, f32[768,256]{1,0:T(8,128)}, bf16[8,768,256]{2,1,0:T(8,128)(2,1)}, s32[8,8,128]{2,1,0:T(8,128)}) custom-call(bf16[3072,256]{1,0:T(8,128)(2,1)} %features.1, bf16[256,256]{1,0:T(8,128)(2,1)} %w_self.1, bf16[256,256]{1,0:T(8,128)(2,1)} %w_neigh.1, ...), custom_call_target="tpu_custom_call" | custom-call | tf_op jit(solution)/shard_map/pallas_call | solution.py:390
  64.4 1.4 slice.26
  65.8 12.1 %shard_map.112 = (bf16[768,256]{1,0:T(8,128)(2,1)}, bf16[768,256]{1,0:T(8,128)(2,1)}, bf16[8,768,256]{2,1,0:T(8,128)(2,1)}) custom-call(s32[6,4]{1,0:T(8,128)} %copy.13.local_refs, s32[6,16]{1,0:T(8,128)} %remote_refs.1, s32[8,12]{1,0:T(8,128)} %bitcast.6, bf16[6,20,128,128]{3,2,1,0:T(8,128)(2,1)} %weights.1, f32[768,256]{1,0:T(8,128)} %get-tuple-element.28.self_part, ...), custom_call_target="tpu_custom_call" | custom-call | tf_op jit(solution)/shard_map/pallas_call | solution.py:411
  77.9 68.0 %shard_map.113 = (bf16[3072,256]{1,0:T(8,128)(2,1)}, f32[256,256]{1,0:T(8,128)}, f32[256,256]{1,0:T(8,128)}) custom-call(bf16[2,2,2,768,256]{4,3,2,1,0:T(8,128)(2,1)} %bitcast.5, bf16[768,256]{1,0:T(8,128)(2,1)} %get-tuple-element.32.grad_self, bf16[4,768,256]{2,1,0:T(8,128)(2,1)} %get-tuple-element.33.own, bf16[4,256,512]{2,1,0:T(8,128)(2,1)} %get-tuple-element.34.w_full), custom_call_target="tpu_custom_call" | custom-call | tf_op jit(solution)/shard_map/pallas_call | solution.py:439
  145.9 0.0 copy-start.1
  145.9 0.0 copy-start
  145.9 2.7 %copy.17 = bf16[3072,256]{1,0:T(8,128)(2,1)} copy(bf16[3072,256]{1,0:T(8,128)(2,1)} %get-tuple-element.43) | data formatting | bytes 3145728
  148.6 0.0 copy-done.1
  148.6 0.7 copy.18
  149.3 0.0 copy-done
  149.3 0.7 copy.19
Async XLA Ops:
  145.9 2.7 %copy-start.1 = (f32[256,256]{1,0:T(8,128)S(1)}, f32[256,256]{1,0:T(8,128)}, u32[]{:S(2)}) copy-start(f32[256,256]{1,0:T(8,128)} %get-tuple-element.44) | copy-start | bytes 786436
  145.9 3.4 %copy-start = (f32[256,256]{1,0:T(8,128)S(1)}, f32[256,256]{1,0:T(8,128)}, u32[]{:S(2)}) copy-start(f32[256,256]{1,0:T(8,128)} %get-tuple-element.45) | copy-start | bytes 786436

commit v2 on v1

--- a/solution.py
+++ b/solution.py
@@ -13,8 +13,9 @@
 BF16 = jnp.bfloat16
 LANES = 8
 HALVES = 2
+PIECES = 6
 ORDERS = 2
-VMEM_LIMIT = 60 * 1024 * 1024
+MIB = 1024 * 1024
 
 
 def send(src, dst, send_sem, recv_sem, where):
@@ -45,6 +46,22 @@
             barrier, inc=1, device_id={"feat": lax.rem(z + i, feat_count)}, device_id_type=MESH
         )
     pl.semaphore_wait(barrier, dom_count + feat_count - 2)
+
+
+def feat_order(z, nf):
+    inner = (z + 1) // 2 % 2
+    half = nf // 2
+    far_first = [*range(half, nf), *range(1, half)]
+    near_first = [*range(1, half), *range(nf - 1, half - 1, -1)]
+    targets = []
+    for far, near in zip(far_first, near_first):
+        mask = inner * far + (1 - inner) * near
+        target, bit = 0, 1
+        while bit < nf:
+            target = target + (z // bit + mask // bit) % 2 * bit
+            bit *= 2
+        targets.append(target)
+    return targets
 
 
 def rows_at(start, size, unit):
@@ -77,8 +94,7 @@
     local = pltpu.make_async_copy(features.at[rows_at(z * rows, rows, rows), :], own.at[z], local_sem)
     local.start()
     for h in range(HALVES):
-        for i in range(nf - 1, 0, -1):
-            zt = lax.rem(z + i, nf)
+        for i, zt in enumerate(feat_order(z, nf)):
             sends.append(send(
                 features.at[rows_at(zt * rows + h * half, half, half), :],
                 own.at[z, pl.ds(h * half, half), :],
@@ -86,8 +102,8 @@
             ))
     for i in range(1, dom_count):
         to = lax.rem(d + i, dom_count)
-        sends.append(send(slots.at[to], table.at[d], ts.at[i], tr.at[d], {"dom": to}))
-    table[d] = slots[d]
+        sends.append(send(slots.at[0], table.at[d], ts.at[i], tr.at[d], {"dom": to}))
+    table[d] = slots[0]
     for i in range(1, nf):
         zs = lax.rem(z + i, nf)
         ref = w_full.at[zs, mine, :]
@@ -186,7 +202,7 @@
         else:
             q = remote_refs[t, k - local_count]
             r = q // slot_count
-            u = table[r, q - r * slot_count]
+            u = table[r, d, q - r * slot_count]
         blocks.append(r)
         spans.append(rows_at(u * tile, tile, tile))
     degree = jnp.zeros((tile, tile), F32)
@@ -226,7 +242,7 @@
 def reduce_kernel(
     sizes, scale, partial, grad_self, own, w_full, grad_out, gw_self, gw_neigh,
     from_sib, sums, b1, b2, grad_proj, stage, gw, gw_recv, gw_sum, gw_cross, gw_z,
-    local_sem, ss, sr, as1, ar1, as2, ar2, zs_, zr, g1s, g1r, gcs, gcr, g2s, g2r, g3s, g3r,
+    ss, sr, as1, ar1, as2, ar2, zs_, zr, g1s, g1r, gcs, gcr, g2s, g2r, g3s, g3r,
 ):
     dom_count, nf, rows, fl, hidden, n = sizes
     d, z = lax.axis_index("dom"), lax.axis_index("feat")
@@ -236,11 +252,11 @@
     lane = lax.rem(d, LANES)
     base = d - lane
     wr = fl // LANES
-    chunks = HALVES * ORDERS
+    chunks = PIECES
     piece = rows // chunks
     groups = dom_count // LANES
     greet(dom_count, nf)
-    sends, locals_ = [], []
+    sends = []
     for c in range(chunks):
         span = pl.ds(c * piece, piece)
         sends.append(send(
@@ -248,7 +264,9 @@
             ss.at[c], sr.at[c], {"dom": chip * 2 + 1 - core},
         ))
     grad_proj[:, :hidden] = grad_self[...]
-    for c in range(chunks):
+    order = feat_order(z, nf)
+
+    def combine(c):
         span = pl.ds(c * piece, piece)
         arrived(from_sib.at[:, :, span, :], sr.at[c])
         for yy in range(n):
@@ -265,13 +283,14 @@
                 yt = lax.rem(y + i, n)
                 src, me, to = sums.at[yt, :, span, :], y, (yt * n + x) * 2 + core
             sends.append(send(src, b1.at[me, :, span, :], as1.at[c, i], ar1.at[c, me], {"dom": to}))
-    for c in range(chunks):
+
+    def turn(c):
         span = pl.ds(c * piece, piece)
         me1, me2 = (x, y) if c % ORDERS == 0 else (y, x)
         for i in range(1, n):
             other = lax.rem(me1 + i, n)
             arrived(b1.at[other, :, span, :], ar1.at[c, other])
-        for j in range(n):
+        for j in [*range(1, n), 0]:
             to2 = lax.rem(me2 + j, n)
             if c % ORDERS == 0:
                 total = sums[to2, x, span, :].astype(F32)
@@ -286,7 +305,8 @@
                     b1.at[me1, to2, span, :], b2.at[me2, span, :], as2.at[c, j], ar2.at[c, me2],
                     {"dom": to},
                 ))
-    for c in range(chunks):
+
+    def settle(c):
         span = pl.ds(c * piece, piece)
         me1, me2 = (x, y) if c % ORDERS == 0 else (y, x)
         total = b1[me1, me2, span, :].astype(F32)
@@ -295,25 +315,46 @@
             arrived(b2.at[other, span, :], ar2.at[c, other])
             total += b2[other, span, :].astype(F32)
         grad_proj[span, hidden:] = total.astype(BF16)
-        for i in range(nf - 1, -1, -1):
-            zt = lax.rem(z + i, nf)
-            stage[zt, span, :] = lax.dot_general(
-                grad_proj[span, :], w_full[zt], (((1,), (1,)), ((), ())),
+
+    def feature_rows(c, zt):
+        span = pl.ds(c * piece, piece)
+        return lax.dot_general(
+            grad_proj[span, :], w_full[zt], (((1,), (1,)), ((), ())),
+            preferred_element_type=F32,
+        ).astype(BF16)
+
+    def deliver(c):
+        span = pl.ds(c * piece, piece)
+        for i, zt in enumerate(order):
+            stage[zt, span, :] = feature_rows(c, zt)
+            sends.append(send(
+                stage.at[zt, span, :],
+                grad_out.at[rows_at(z * rows + c * piece, piece, piece), :],
+                zs_.at[c, i], zr.at[c, z], {"feat": zt},
+            ))
+
+    def weigh(columns):
+        for k in range(nf):
+            gw[k, :, columns] = lax.dot_general(
+                own[k], grad_proj[:, columns], (((0,), (0,)), ((), ())),
                 preferred_element_type=F32,
             ).astype(BF16)
-            target = grad_out.at[rows_at(z * rows + c * piece, piece, piece), :]
-            if i:
-                sends.append(send(
-                    stage.at[zt, span, :], target, zs_.at[c, i], zr.at[c, z], {"feat": zt}
-                ))
-            else:
-                copy = pltpu.make_async_copy(stage.at[zt, span, :], target, local_sem.at[c])
-                copy.start()
-                locals_.append(copy)
-    for k in range(nf):
-        gw[k] = lax.dot_general(
-            own[k], grad_proj[...], (((0,), (0,)), ((), ())), preferred_element_type=F32
-        ).astype(BF16)
+
+    plan = []
+    for c in range(chunks + 2):
+        if c < chunks:
+            plan.append((combine, c))
+        if 1 <= c <= chunks:
+            plan.append((turn, c - 1))
+        if c >= 2:
+            plan.append((settle, c - 2))
+            if c - 2 < chunks - 1:
+                plan.append((deliver, c - 2))
+        if c == 0:
+            plan.append((weigh, slice(0, hidden)))
+    for step, what in plan:
+        step(what)
+    weigh(slice(hidden, 2 * hidden))
     mine = rows_at(lane * wr, wr, wr)
     for j in range(1, LANES):
         other = lax.rem(lane + j, LANES)
@@ -343,6 +384,9 @@
     for i in range(1, nf):
         zt = lax.rem(z + i, nf)
         sends.append(send(gw_sum.at[zt], gw_z.at[z], g2s.at[i], g2r.at[z], {"feat": zt}))
+    deliver(chunks - 1)
+    for c in range(chunks):
+        grad_out[rows_at(z * rows + c * piece, piece, piece), :] = feature_rows(c, z)
     final = gw_sum[z]
     for i in range(1, nf):
         zt = lax.rem(z + i, nf)
@@ -364,8 +408,6 @@
         for i in range(1, nf):
             zt = lax.rem(z + i, nf)
             arrived(grad_out.at[rows_at(zt * rows + c * piece, piece, piece), :], zr.at[c, zt])
-    for copy in locals_:
-        copy.wait()
     for copy in sends:
         copy.wait_send()
 
@@ -381,12 +423,12 @@
     chips = n * n
     chunks = HALVES * ORDERS
     node_total = rows * dom_count * nf
+    vmem_limit = min(60, 8 + 2 * dom_count) * MIB
     vmem = pl.BlockSpec(memory_space=pltpu.VMEM)
     smem = pl.BlockSpec(memory_space=pltpu.SMEM)
     hbm = pl.BlockSpec(memory_space=pl.ANY)
     dma = pltpu.SemaphoreType.DMA
     sizes = (dom_count, nf, rows, fl, hidden, n)
-    slots = jnp.zeros((dom_count, 8, 128), jnp.int32).at[:, 0, :slot_count].set(send_tiles[0])
     own, w_full, self_part, gathered, table = pl.pallas_call(
         functools.partial(project_kernel, sizes),
         out_shape=(
@@ -394,7 +436,7 @@
             jax.ShapeDtypeStruct((nf, fl, 2 * hidden), BF16),
             jax.ShapeDtypeStruct((rows, hidden), F32),
             jax.ShapeDtypeStruct((dom_count, rows, hidden), BF16),
-            jax.ShapeDtypeStruct((dom_count, 8, 128), jnp.int32),
+            jax.ShapeDtypeStruct((dom_count, dom_count, slot_count), jnp.int32),
         ),
         in_specs=[hbm, vmem, vmem, vmem],
         out_specs=(vmem,) * 5,
@@ -404,9 +446,9 @@
             dma((chunks, n)), dma((chunks, n, n)), dma((chunks, n, n)), dma((dom_count, chunks)),
         ],
         compiler_params=pltpu.CompilerParams(
-            collective_id=0, has_side_effects=True, vmem_limit_bytes=VMEM_LIMIT
-        ),
-    )(features, w_self, w_neigh, slots)
+            collective_id=0, has_side_effects=True, vmem_limit_bytes=vmem_limit
+        ),
+    )(features, w_self, w_neigh, send_tiles)
 
     hidden_out, grad_self, partial = pl.pallas_call(
         functools.partial(
@@ -431,8 +473,8 @@
             vmem,
         ),
         scratch_shapes=[pltpu.VMEM((dom_count, rows, hidden), F32)],
-        compiler_params=pltpu.CompilerParams(vmem_limit_bytes=VMEM_LIMIT),
-    )(local_refs, remote_refs, table[:, 0, :slot_count], tile_weights, self_part, out_grad, gathered)
+        compiler_params=pltpu.CompilerParams(vmem_limit_bytes=vmem_limit),
+    )(local_refs, remote_refs, table, tile_weights, self_part, out_grad, gathered)
 
     wr = fl // LANES
     groups = dom_count // LANES
@@ -444,7 +486,7 @@
             jax.ShapeDtypeStruct((fl, hidden), F32),
         ),
         in_specs=[vmem] * 4,
-        out_specs=(hbm, vmem, vmem),
+        out_specs=(vmem,) * 3,
         scratch_shapes=[
             pltpu.VMEM((n, n, rows, hidden), BF16),
             pltpu.VMEM((n, n, rows, hidden), BF16),
@@ -457,14 +499,14 @@
             pltpu.VMEM((nf, wr, 2 * hidden), F32),
             pltpu.VMEM((groups, nf, wr, 2 * hidden), F32),
             pltpu.VMEM((nf, wr, 2 * hidden), F32),
-            dma((chunks,)), dma((chunks,)), dma((chunks,)),
-            dma((chunks, n)), dma((chunks, n)), dma((chunks, n)), dma((chunks, n)),
-            dma((chunks, nf)), dma((chunks, nf)),
+            dma((PIECES,)), dma((PIECES,)),
+            dma((PIECES, n)), dma((PIECES, n)), dma((PIECES, n)), dma((PIECES, n)),
+            dma((PIECES, nf)), dma((PIECES, nf)),
             dma((LANES,)), dma((LANES,)), dma((groups,)), dma((groups,)),
             dma((nf,)), dma((nf,)), dma((2, LANES)), dma((2, LANES)),
         ],
         compiler_params=pltpu.CompilerParams(
-            collective_id=1, has_side_effects=True, vmem_limit_bytes=VMEM_LIMIT
+            collective_id=1, has_side_effects=True, vmem_limit_bytes=vmem_limit
         ),
     )(partial.reshape(2, n, n, rows, hidden), grad_self, own, w_full)
     return (hidden_out, grad_out, gw_self, gw_neigh)

time: 150 us -> 133 us (0.89)
  Pallas kernels: 141 us -> 122 us
    pallas_call x1, Pallas kernels: 68 us -> 59.2 us  [body(): pl.pallas_call(functools.partial(reduce_kernel, sizes, float(node_total)...]
    pallas_call x1, Pallas kernels: 61.1 us -> 52.6 us  [body(): pl.pallas_call(functools.partial(project_kernel, sizes), out_shape=(jax.S...]
    unnamed x8 -> x18, local copies, waits for them, and re-layouts: 5.47 us -> 9.34 us
    pallas_call x1, Pallas kernels: 12.1 us -> 10 us  [body(): pl.pallas_call(functools.partial(aggregate_kernel, (dom_count, local_coun...]
where the time goes in v2:
time: 133 us; the launch traced here: 132 us
  Pallas kernels  122 us (92%)
  local copies, waits for them, and re-layouts  9.34 us (7%)
    pallas_call x1, Pallas kernels, body(): pl.pallas_call(functools.partial(reduce_kernel, sizes, float(node_total)...  59.2 us
    pallas_call x1, Pallas kernels, body(): pl.pallas_call(functools.partial(project_kernel, sizes), out_shape=(jax.S...  52.6 us
    pallas_call x1, Pallas kernels, body(): pl.pallas_call(functools.partial(aggregate_kernel, (dom_count, local_coun...  10 us
    unnamed x18, local copies, waits for them, and re-layouts  9.34 us

profile of v2, /device:TPU:0, one launch (start us, length us, event | category | flops | bytes accessed | tf_op | source)
XLA Modules:
  0.0 131.9 jit_solution(6346758225706795166)
XLA Ops:
  0.6 0.0 copy-start.6
  0.6 0.8 copy.12.local_refs
  1.4 0.0 copy-start.1
  1.4 1.4 %copy-done.1 = bf16[3072,256]{1,0:T(8,128)(2,1)S(1)} copy-done((bf16[3072,256]{1,0:T(8,128)(2,1)S(1)}, bf16[3072,256]{1,0:T(8,128)(2,1)}, u32[]{:S(2)}) %copy-start.1) | copy-done | bytes 1572888
  2.8 0.0 copy-start.3
  2.8 0.9 copy-done.3
  3.7 0.0 copy-start.4
  3.7 0.9 copy-done.4
  4.6 0.0 copy-start.5
  4.6 0.7 copy-done.5
  5.3 0.0 copy-start.2
  5.3 52.6 %shard_map.111 = (bf16[4,768,256]{2,1,0:T(8,128)(2,1)S(1)}, bf16[4,256,512]{2,1,0:T(8,128)(2,1)S(1)}, f32[768,256]{1,0:T(8,128)S(1)}, bf16[8,768,256]{2,1,0:T(8,128)(2,1)S(1)}, s32[8,8,12]{2,1,0:T(8,128)S(1)}) custom-call(bf16[3072,256]{1,0:T(8,128)(2,1)S(1)} %copy-done.1, bf16[256,256]{1,0:T(8,128)(2,1)S(1)} %copy-done.3, bf16[256,256]{1,0:T(8,128)(2,1)S(1)} %copy-done.4, ...), custom_call_target="tpu_custom_call" | custom-call | tf_op jit(solution)/shard_map/pallas_call | solution.py:432
  57.9 0.0 copy-done.6
  57.9 0.0 copy-done.2
  57.9 0.0 copy-start
  58.0 2.1 %copy-done = bf16[6,20,128,128]{3,2,1,0:T(8,128)(2,1)S(1)} copy-done((bf16[6,20,128,128]{3,2,1,0:T(8,128)(2,1)S(1)}, bf16[6,20,128,128]{3,2,1,0:T(8,128)(2,1)}, u32[]{:S(2)}) %copy-start) | copy-done | bytes 3932184
  60.1 10.0 %shard_map.112 = (bf16[768,256]{1,0:T(8,128)(2,1)}, bf16[768,256]{1,0:T(8,128)(2,1)S(1)}, bf16[8,768,256]{2,1,0:T(8,128)(2,1)S(1)}) custom-call(s32[6,4]{1,0:T(8,128)S(1)} %copy.12.local_refs, s32[6,16]{1,0:T(8,128)S(1)} %copy-done.6, s32[8,8,12]{2,1,0:T(8,128)S(1)} %get-tuple-element.15.table, bf16[6,20,128,128]{3,2,1,0:T(8,128)(2,1)S(1)} %copy-done, ...), custom_call_target="tpu_custom_call" | custom-call | tf_op jit(solution)/shard_map/pallas_call | solution.py:453
  70.1 59.2 %shard_map.113 = (bf16[3072,256]{1,0:T(8,128)(2,1)S(1)}, f32[256,256]{1,0:T(8,128)S(1)}, f32[256,256]{1,0:T(8,128)S(1)}) custom-call(bf16[2,2,2,768,256]{4,3,2,1,0:T(8,128)(2,1)S(1)} %bitcast.1, bf16[768,256]{1,0:T(8,128)(2,1)S(1)} %get-tuple-element.20.grad_self, bf16[4,768,256]{2,1,0:T(8,128)(2,1)S(1)} %get-tuple-element.21.own, ...), custom_call_target="tpu_custom_call" | custom-call | tf_op jit(solution)/shard_map/pallas_call | solution.py:481
  129.3 1.1 copy.16
  130.5 0.7 copy.17
  131.2 0.7 copy.18
Async XLA Ops:
  0.6 57.3 %copy-start.6 = (s32[6,16]{1,0:T(8,128)S(1)}, s32[6,16]{1,0:T(8,128)}, u32[]{:S(2)}) copy-start(s32[6,16]{1,0:T(8,128)} %remote_refs.1) | copy-start | bytes 1156
  1.4 1.4 %copy-start.1 = (bf16[3072,256]{1,0:T(8,128)(2,1)S(1)}, bf16[3072,256]{1,0:T(8,128)(2,1)}, u32[]{:S(2)}) copy-start(bf16[3072,256]{1,0:T(8,128)(2,1)} %features.1) | copy-start | bytes 4718596
  2.8 0.9 copy-start.3
  3.7 0.9 copy-start.4
  4.6 0.7 copy-start.5
  5.3 52.6 %copy-start.2 = (bf16[768,256]{1,0:T(8,128)(2,1)S(1)}, bf16[768,256]{1,0:T(8,128)(2,1)}, u32[]{:S(2)}) copy-start(bf16[768,256]{1,0:T(8,128)(2,1)} %out_grad.1) | copy-start | bytes 1179652
  57.9 2.1 %copy-start = (bf16[6,20,128,128]{3,2,1,0:T(8,128)(2,1)S(1)}, bf16[6,20,128,128]{3,2,1,0:T(8,128)(2,1)}, u32[]{:S(2)}) copy-start(bf16[6,20,128,128]{3,2,1,0:T(8,128)(2,1)} %weights.1) | copy-start | bytes 11796484

commit v3 on v2

--- a/solution.py
+++ b/solution.py
@@ -348,7 +348,7 @@
             plan.append((turn, c - 1))
         if c >= 2:
             plan.append((settle, c - 2))
-            if c - 2 < chunks - 1:
+            if c - 2 < chunks - 2:
                 plan.append((deliver, c - 2))
         if c == 0:
             plan.append((weigh, slice(0, hidden)))
@@ -384,6 +384,7 @@
     for i in range(1, nf):
         zt = lax.rem(z + i, nf)
         sends.append(send(gw_sum.at[zt], gw_z.at[z], g2s.at[i], g2r.at[z], {"feat": zt}))
+    deliver(chunks - 2)
     deliver(chunks - 1)
     for c in range(chunks):
         grad_out[rows_at(z * rows + c * piece, piece, piece), :] = feature_rows(c, z)

time: 133 us -> 132 us (level)
  no operation moved by 1% of the time
where the time goes in v3:
time: 132 us
  Pallas kernels  122 us (92%)
  local copies, waits for them, and re-layouts  9.34 us (7%)
    pallas_call x1, Pallas kernels, body(): pl.pallas_call(functools.partial(reduce_kernel, sizes, float(node_total)...  59.3 us
    pallas_call x1, Pallas kernels, body(): pl.pallas_call(functools.partial(project_kernel, sizes), out_shape=(jax.S...  52.6 us
    pallas_call x1, Pallas kernels, body(): pl.pallas_call(functools.partial(aggregate_kernel, (dom_count, local_coun...  10 us
    unnamed x18, local copies, waits for them, and re-layouts  9.34 us

profile of v3, /device:TPU:0, one launch (start us, length us, event | category | flops | bytes accessed | tf_op | source)
XLA Modules:
  0.0 132.0 jit_solution(8227180770064977286)
XLA Ops:
  0.6 0.0 copy-start.6
  0.6 0.8 copy.12.local_refs
  1.4 0.0 copy-start.1
  1.4 1.4 %copy-done.1 = bf16[3072,256]{1,0:T(8,128)(2,1)S(1)} copy-done((bf16[3072,256]{1,0:T(8,128)(2,1)S(1)}, bf16[3072,256]{1,0:T(8,128)(2,1)}, u32[]{:S(2)}) %copy-start.1) | copy-done | bytes 1572888
  2.8 0.0 copy-start.3
  2.8 0.9 copy-done.3
  3.7 0.0 copy-start.4
  3.7 0.9 copy-done.4
  4.6 0.0 copy-start.5
  4.6 0.7 copy-done.5
  5.3 0.0 copy-start.2
  5.3 52.6 %shard_map.111 = (bf16[4,768,256]{2,1,0:T(8,128)(2,1)S(1)}, bf16[4,256,512]{2,1,0:T(8,128)(2,1)S(1)}, f32[768,256]{1,0:T(8,128)S(1)}, bf16[8,768,256]{2,1,0:T(8,128)(2,1)S(1)}, s32[8,8,12]{2,1,0:T(8,128)S(1)}) custom-call(bf16[3072,256]{1,0:T(8,128)(2,1)S(1)} %copy-done.1, bf16[256,256]{1,0:T(8,128)(2,1)S(1)} %copy-done.3, bf16[256,256]{1,0:T(8,128)(2,1)S(1)} %copy-done.4, ...), custom_call_target="tpu_custom_call" | custom-call | tf_op jit(solution)/shard_map/pallas_call | solution.py:433
  57.9 0.0 copy-done.6
  57.9 0.0 copy-done.2
  57.9 0.0 copy-start
  58.0 2.1 %copy-done = bf16[6,20,128,128]{3,2,1,0:T(8,128)(2,1)S(1)} copy-done((bf16[6,20,128,128]{3,2,1,0:T(8,128)(2,1)S(1)}, bf16[6,20,128,128]{3,2,1,0:T(8,128)(2,1)}, u32[]{:S(2)}) %copy-start) | copy-done | bytes 3932184
  60.1 10.0 %shard_map.112 = (bf16[768,256]{1,0:T(8,128)(2,1)}, bf16[768,256]{1,0:T(8,128)(2,1)S(1)}, bf16[8,768,256]{2,1,0:T(8,128)(2,1)S(1)}) custom-call(s32[6,4]{1,0:T(8,128)S(1)} %copy.12.local_refs, s32[6,16]{1,0:T(8,128)S(1)} %copy-done.6, s32[8,8,12]{2,1,0:T(8,128)S(1)} %get-tuple-element.15.table, bf16[6,20,128,128]{3,2,1,0:T(8,128)(2,1)S(1)} %copy-done, ...), custom_call_target="tpu_custom_call" | custom-call | tf_op jit(solution)/shard_map/pallas_call | solution.py:454
  70.1 59.3 %shard_map.113 = (bf16[3072,256]{1,0:T(8,128)(2,1)S(1)}, f32[256,256]{1,0:T(8,128)S(1)}, f32[256,256]{1,0:T(8,128)S(1)}) custom-call(bf16[2,2,2,768,256]{4,3,2,1,0:T(8,128)(2,1)S(1)} %bitcast.1, bf16[768,256]{1,0:T(8,128)(2,1)S(1)} %get-tuple-element.20.grad_self, bf16[4,768,256]{2,1,0:T(8,128)(2,1)S(1)} %get-tuple-element.21.own, ...), custom_call_target="tpu_custom_call" | custom-call | tf_op jit(solution)/shard_map/pallas_call | solution.py:482
  129.4 1.1 copy.16
  130.6 0.7 copy.17
  131.3 0.7 copy.18
Async XLA Ops:
  0.6 57.3 %copy-start.6 = (s32[6,16]{1,0:T(8,128)S(1)}, s32[6,16]{1,0:T(8,128)}, u32[]{:S(2)}) copy-start(s32[6,16]{1,0:T(8,128)} %remote_refs.1) | copy-start | bytes 1156
  1.4 1.4 %copy-start.1 = (bf16[3072,256]{1,0:T(8,128)(2,1)S(1)}, bf16[3072,256]{1,0:T(8,128)(2,1)}, u32[]{:S(2)}) copy-start(bf16[3072,256]{1,0:T(8,128)(2,1)} %features.1) | copy-start | bytes 4718596
  2.8 0.9 copy-start.3
  3.7 0.9 copy-start.4
  4.6 0.7 copy-start.5
  5.3 52.6 %copy-start.2 = (bf16[768,256]{1,0:T(8,128)(2,1)S(1)}, bf16[768,256]{1,0:T(8,128)(2,1)}, u32[]{:S(2)}) copy-start(bf16[768,256]{1,0:T(8,128)(2,1)} %out_grad.1) | copy-start | bytes 1179652
  57.9 2.1 %copy-start = (bf16[6,20,128,128]{3,2,1,0:T(8,128)(2,1)S(1)}, bf16[6,20,128,128]{3,2,1,0:T(8,128)(2,1)}, u32[]{:S(2)}) copy-start(bf16[6,20,128,128]{3,2,1,0:T(8,128)(2,1)} %weights.1) | copy-start | bytes 11796484
